TPU v7x, 512 devices: a whole 4x8x8 slice. The times are simulated.
512 devices in a mesh: dp: 32 (over x, y), tensor: 16 (over z, core).
Axes of the slice: x: 4, y: 8, z: 8, core: 2. Of those that a mesh axis runs over, the one named last changes fastest.
Arguments:
- queries: bfloat16 [128, 4, 128, 128], P('dp', None, 'tensor'), parts along dimension 0, may hold values from -18 to 18
- cache: bfloat16 [16, 128, 256, 256], P('tensor', 'dp'), parts along dimension 1, may hold values from -10 to 10
- new_kv: bfloat16 [16, 128, 4, 256], P('tensor', 'dp'), parts along dimension 1, may hold values from -6 to 6
- cache_len: int32 [128], P('dp'), parts along dimension 0, may hold values from 64 to 256, as said below
- target_logits: bfloat16 [512, 128256], P('dp', 'tensor'), parts along dimension 0, may hold values from -19 to 262
- drafter: bfloat16 [512, 2, 16, 8016], P(('dp', 'tensor')), parts along dimension 0, may hold values from 0.0009 to 3.01, as said below
- draft_tokens: int32 [512], P('dp'), parts along dimension 0, may hold values from 0 to 128255
- language: int32 [128], P('dp'), parts along dimension 0, may hold values from 0 to 1
- uniforms: float32 [512], P('dp'), parts along dimension 0, may hold values from 0 to 1
Outputs:
- attn_out: bfloat16 [128, 4, 128, 128], P('dp', None, 'tensor'), parts along dimension 0
- accept_margin: float32 [512], P('dp'), parts along dimension 0
- residual_mass: float32 [512], P('dp'), parts along dimension 0
There are 32 independent parts, one for each index of `dp`. A program takes and returns all parts, laid end to end along the dimension named above; each array names one. Nothing has to cross between parts.
Inputs may be any that keep to these rules, and one draw needn't show every extreme that they name: `cache_len`: every request has 64 or more positions in use; some request has exactly 256. `drafter`: entries are positive.
All inputs are finite; a program needn't handle non-finite values.
Results may differ from a plain program's by a relative error of at most 0.0049.
Values may be sent and summed in bfloat16 or wider, within the bound.
A program may use at most 64 MiB of HBM per device.

v0:
```python
import math

import jax
import jax.numpy as jnp
from jax import lax
from jax.sharding import PartitionSpec as P

DRAFTS = 4


NEGATIVE = -1e30


def attend(queries, cache, new_kv, cache_len):
    row_count, drafts, heads_here, head_depth = queries.shape
    slots_here = cache.shape[0]
    group_size = heads_here // slots_here
    grouped = queries.reshape(row_count, drafts, slots_here, group_size, head_depth)
    score_scale = 1.0 / math.sqrt(head_depth)
    past_scores = (
        jnp.einsum(
            "rigkd,grtd->rgikt",
            grouped,
            cache[..., :head_depth],
            preferred_element_type=jnp.float32,
        )
        * score_scale
    )
    fresh_scores = (
        jnp.einsum(
            "rigkd,grjd->rgikj",
            grouped,
            new_kv[..., :head_depth],
            preferred_element_type=jnp.float32,
        )
        * score_scale
    )
    past_pos = lax.broadcasted_iota(jnp.int32, (row_count, 1, 1, 1, cache.shape[2]), 4)
    past_ok = past_pos < cache_len.reshape(row_count, 1, 1, 1, 1)
    fresh_key = lax.broadcasted_iota(jnp.int32, (1, 1, drafts, 1, drafts), 4)
    fresh_query = lax.broadcasted_iota(jnp.int32, (1, 1, drafts, 1, drafts), 2)
    past_scores = jnp.where(past_ok, past_scores, -jnp.inf)
    fresh_scores = jnp.where(fresh_key <= fresh_query, fresh_scores, -jnp.inf)
    row_peak = jnp.maximum(
        jnp.max(past_scores, axis=4, keepdims=True), jnp.max(fresh_scores, axis=4, keepdims=True)
    )
    past_exp = jnp.exp(past_scores - row_peak)
    fresh_exp = jnp.exp(fresh_scores - row_peak)
    exp_total = jnp.sum(past_exp, axis=4, keepdims=True) + jnp.sum(fresh_exp, axis=4, keepdims=True)
    past_w = (past_exp / exp_total).astype(jnp.bfloat16)
    fresh_w = (fresh_exp / exp_total).astype(jnp.bfloat16)
    mixed = jnp.einsum(
        "rgikt,grtd->rigkd", past_w, cache[..., head_depth:], preferred_element_type=jnp.float32
    )
    mixed = mixed + jnp.einsum(
        "rgikj,grjd->rigkd", fresh_w, new_kv[..., head_depth:], preferred_element_type=jnp.float32
    )
    return mixed.reshape(row_count, drafts, heads_here, head_depth).astype(jnp.bfloat16)


def pick_language(options, slot_lang):
    chosen = options[0]
    chosen = jnp.where(slot_lang[:, None] == 1, options[1], chosen)
    return chosen


def on_device(
    queries, cache, new_kv, cache_len, target_logits, drafter, draft_tokens, language, uniforms
):
    attn_out = attend(queries, cache, new_kv, cache_len)
    tensor_rank = lax.axis_index("tensor")
    slot_lang = jnp.repeat(language, DRAFTS)
    slot_share, lang_count, piece_count, vocab_share = drafter.shape
    total_slots = slot_share * piece_count
    offset = tensor_rank * vocab_share
    arrived = lax.all_to_all(drafter, "tensor", split_axis=2, concat_axis=2, tiled=True)
    options = arrived.transpose(1, 2, 0, 3).reshape(lang_count, total_slots, vocab_share)
    chosen = pick_language(options, slot_lang)
    logits = target_logits.astype(jnp.float32)
    column = lax.broadcasted_iota(jnp.int32, logits.shape, 1) + offset
    marked = column == draft_tokens[:, None]
    draft_weights = chosen.astype(jnp.float32)
    local_peak = jnp.max(logits, axis=1)
    local_draft = jnp.max(jnp.where(marked, logits, NEGATIVE), axis=1)
    weight_local = jnp.sum(draft_weights, axis=1)
    weight_draft_local = jnp.sum(jnp.where(marked, draft_weights, 0.0), axis=1)
    row_peak, draft_logit = lax.pmax((local_peak, local_draft), "tensor")
    exp_terms = jnp.exp(logits - row_peak[:, None])
    norm_total, weight_total, weight_draft = lax.psum(
        (jnp.sum(exp_terms, axis=1), weight_local, weight_draft_local), "tensor"
    )
    target_probs = exp_terms / norm_total[:, None]
    drafted = draft_weights / weight_total[:, None]
    residual_mass = lax.psum(jnp.sum(jnp.maximum(target_probs - drafted, 0.0), axis=1), "tensor")
    draft_prob = jnp.exp(draft_logit - row_peak) / norm_total
    draft_share = weight_draft / weight_total
    accept_margin = jnp.minimum(1.0, draft_prob / draft_share) - uniforms
    return (attn_out, accept_margin, residual_mass)


def solution(mesh):
    in_specs = (
        P("dp", None, "tensor", None),
        P("tensor", "dp", None, None),
        P("tensor", "dp", None, None),
        P("dp"),
        P("dp", "tensor"),
        P(("dp", "tensor"), None, None, None),
        P("dp"),
        P("dp"),
        P("dp"),
    )
    out_specs = (P("dp", None, "tensor", None), P("dp"), P("dp"))
    return jax.shard_map(
        on_device, mesh=mesh, in_specs=in_specs, out_specs=out_specs, check_vma=False
    )
```

profile of v0, /device:TPU:1, one launch (start us, length us, event | category | flops | bytes accessed | tf_op | source)
XLA Modules:
  0.0 123.4 jit_solution(8764828491974696211)
XLA Ops:
  0.6 0.0 copy-start
  0.6 2.2 %copy.14 = bf16[1,2,16,8016]{3,1,0,2:T(2,128)(2,1)} copy(bf16[1,2,16,8016]{3,2,1,0:T(8,128)(2,1)} %param.14) | data formatting | bytes 1026048 | tf_op args[5]
  2.9 0.0 copy-start.1
  2.9 12.0 %all-to-all-start = ((bf16[1,2,16,8016]{3,1,0,2:T(2,128)(2,1)}), bf16[1,2,16,8016]{3,1,0,2:T(2,128)(2,1)S(1)}, u32[]{:S(2)}, u32[]{:S(2)}) async-start(bf16[1,2,16,8016]{3,1,0,2:T(2,128)(2,1)} %copy.14), calls=%async_computation | async-start | bytes 1032192 | tf_op jit(solution)/shard_map/all_to_all | solution.py:76
  14.9 0.6 copy-done.6
  15.5 0.1 iota_compare_fusion
  15.6 0.0 copy-done.1
  15.6 0.2 reduce_max.44
  15.8 0.0 copy-done
  15.8 0.0 copy-done.2
  15.8 0.0 copy-start.5
  15.8 0.3 fusion.29
  16.1 0.4 copy-done.5
  16.5 0.3 fusion.30
  16.7 0.4 copy-done.7
  17.1 29.0 %pmax.15 = f32[16]{0:T(128)S(1)} all-reduce(bf16[16]{0:T(256)(128)(2,1)S(1)} %reduce_max.44), channel_id=1, replica_groups=mesh['dp'=32,'tensor'=16] {'tensor'}, use_global_device_ids=true, to_apply=%region_7.8 | all-reduce | flops 16 | bytes 96 | tf_op jit(solution)/shard_map/pmax | solution.py:87
  46.1 0.1 broadcast_in_dim.55
  46.2 0.1 eq.23
  46.3 0.2 fusion.17
  46.5 0.3 fusion.5
  46.8 0.2 fusion.11
  47.1 0.8 fusion.1
  47.9 0.0 all-to-all-done
  47.9 0.7 fusion.28
  48.6 0.4 convert_reduce_fusion
  49.0 24.4 %all-reduce.1 = (f32[16]{0:T(128)S(1)}, f32[16]{0:T(128)S(1)}) all-reduce(f32[16]{0:T(128)S(1)} %fusion.5, f32[16]{0:T(128)S(1)} %get-tuple-element.10), channel_id=1, replica_groups=mesh['dp'=32,'tensor'=16] {'tensor'}, use_global_device_ids=true, to_apply=%region_11.12 | all-reduce | flops 32 | bytes 256 | tf_op jit(solution)/shard_map/psum | solution.py:89
  73.4 0.7 copy-done.3
  74.1 0.5 fusion.10
  74.6 23.5 %pmax.14 = f32[16]{0:T(128)S(1)} all-reduce(f32[16]{0:T(128)S(1)} %get-tuple-element.4), channel_id=1, replica_groups=mesh['dp'=32,'tensor'=16] {'tensor'}, use_global_device_ids=true, to_apply=%region_5.6 | all-reduce | flops 16 | bytes 128 | tf_op jit(solution)/shard_map/pmax | solution.py:87
  98.1 24.0 %all-reduce = (f32[16]{0:T(128)S(1)}, f32[16]{0:T(128)}) all-reduce(f32[16]{0:T(128)S(1)} %get-tuple-element.5, f32[16]{0:T(128)S(1)} %get-tuple-element.3), channel_id=1, replica_groups=mesh['dp'=32,'tensor'=16] {'tensor'}, use_global_device_ids=true, to_apply=%region_13.14 | all-reduce | flops 32 | bytes 256 | tf_op jit(solution)/shard_map/psum | solution.py:89
  122.2 0.7 copy-done.4
  122.8 0.5 minimum_subtract_fusion
  (11 shorter events, 0.1 us)
Async XLA Ops:
  0.6 15.1 %copy-start = (bf16[4,4,8,128]{3,2,1,0:T(8,128)(2,1)S(1)}, bf16[4,4,8,128]{3,2,1,0:T(8,128)(2,1)}, u32[]{:S(2)}) copy-start(bf16[4,4,8,128]{3,2,1,0:T(8,128)(2,1)} %param.9) | copy-start | bytes 98308
  2.9 12.7 %copy-start.1 = (bf16[16,8016]{1,0:T(8,128)(2,1)S(1)}, bf16[16,8016]{1,0:T(8,128)(2,1)}, u32[]{:S(2)}) copy-start(bf16[16,8016]{1,0:T(8,128)(2,1)} %param.13) | copy-start | bytes 769540
  2.9 12.9 %copy-start.2 = (bf16[1,4,256,256]{3,2,1,0:T(8,128)(2,1)S(1)}, bf16[1,4,256,256]{3,2,1,0:T(8,128)(2,1)}, u32[]{:S(2)}) copy-start(bf16[1,4,256,256]{3,2,1,0:T(8,128)(2,1)} %param.10) | copy-start | bytes 1572868
  2.9 45.0 %all-to-all-start = ((bf16[1,2,16,8016]{3,1,0,2:T(2,128)(2,1)}), bf16[1,2,16,8016]{3,1,0,2:T(2,128)(2,1)S(1)}, u32[]{:S(2)}, u32[]{:S(2)}) async-start(bf16[1,2,16,8016]{3,1,0,2:T(2,128)(2,1)} %copy.14), calls=%async_computation | async-start | bytes 1032192 | tf_op jit(solution)/shard_map/all_to_all | solution.py:76
  14.8 0.7 copy-start.6
  15.8 0.7 copy-start.5
  16.5 0.7 copy-start.7
  73.4 0.7 copy-start.3
  122.2 0.7 copy-start.4
where the time goes:
time: 124 us; the launch traced here: 123 us
  blocking collectives  101 us (81%)
  starting transfers between devices  12 us (10%)
  local copies, waits for them, and re-layouts  5.86 us (5%)
  other arithmetic  2.22 us (2%)
  matrix products  1.6 us (1%)
    pmax x2, blocking collectives, on_device(): row_peak, draft_logit = lax.pmax((local_peak, local_draft), 'tensor')  52.5 us
    psum x2, blocking collectives, on_device(): lax.psum((jnp.sum(exp_terms, axis=1), weight_local, weight_draft_local),...  48.5 us
    all_to_all x1, starting transfers between devices, on_device(): lax.all_to_all(drafter, 'tensor', split_axis=2, concat_axis=2, tiled=True)  12 us
    unnamed x17, local copies, waits for them, and re-layouts  4.98 us
  transfers between devices with their start and end apart: 1, of which 0 were waited for; matrix products, arithmetic and copies ran while one was open for 2% of the time, Pallas kernels for 0%

commit v1 on v0

v1 whole, which is shorter than its diff:
```python
import math

import jax
import jax.numpy as jnp
from jax import lax
from jax.experimental import pallas as pl
from jax.experimental.pallas import tpu as pltpu
from jax.sharding import PartitionSpec as P

MESH = pl.DeviceIdType.MESH
GROUP = 16
LANES = 128
VSHARD = 8016
FULL = VSHARD // LANES
TAIL = VSHARD - FULL * LANES
CHUNKS = 64
ABSENT = -3.0e38
ORDER = (8, 9, 7, 10, 6, 11, 5, 12, 4, 13, 3, 14, 2, 15, 1)


def spread(load, tiles, fill):
    for c in range(FULL):
        tiles[pl.ds(GROUP * c, GROUP), :] = load(c * LANES, LANES).astype(jnp.float32)
    rest = (CHUNKS - FULL) * GROUP
    tiles[pl.ds(GROUP * FULL, rest), :] = jnp.full((rest, LANES), fill, jnp.float32)
    tiles[pl.ds(GROUP * FULL, GROUP), 0:TAIL] = load(FULL * LANES, TAIL).astype(jnp.float32)


def attend(r, q, kv, fresh, used):
    depth = q.shape[-1]
    scale = 1.0 / math.sqrt(depth)
    query = q[r].astype(jnp.float32).reshape(32, depth).astype(jnp.bfloat16)
    nt = (((1,), (1,)), ((), ()))
    nn = (((1,), (0,)), ((), ()))
    past = kv[0, r]
    new = fresh[0, r]
    past_scores = (
        lax.dot_general(query, past[:, :depth], nt, preferred_element_type=jnp.float32) * scale
    )
    new_scores = (
        lax.dot_general(query, new[:, :depth], nt, preferred_element_type=jnp.float32) * scale
    )
    position = lax.broadcasted_iota(jnp.int32, past_scores.shape, 1)
    past_scores = jnp.where(position < used, past_scores, -jnp.inf)
    draft = lax.broadcasted_iota(jnp.int32, new_scores.shape, 0) // 8
    key = lax.broadcasted_iota(jnp.int32, new_scores.shape, 1)
    new_scores = jnp.where(key <= draft, new_scores, -jnp.inf)
    peak = jnp.maximum(
        jnp.max(past_scores, axis=1, keepdims=True), jnp.max(new_scores, axis=1, keepdims=True)
    )
    past_exp = jnp.exp(past_scores - peak)
    new_exp = jnp.exp(new_scores - peak)
    total = jnp.sum(past_exp, axis=1, keepdims=True) + jnp.sum(new_exp, axis=1, keepdims=True)
    past_w = (past_exp / total).astype(jnp.bfloat16)
    new_w = (new_exp / total).astype(jnp.bfloat16)
    mixed = lax.dot_general(past_w, past[:, depth:], nn, preferred_element_type=jnp.float32)
    mixed = mixed + lax.dot_general(new_w, new[:, depth:], nn, preferred_element_type=jnp.float32)
    return mixed.reshape(4, 8, depth).astype(jnp.bfloat16)


def kernel(
    q_in,
    kv_in,
    fresh_in,
    used_in,
    logits_in,
    drafter_in,
    token_in,
    language_in,
    uniform_in,
    attn_out,
    margin_out,
    mass_out,
    q,
    kv,
    fresh,
    logits,
    drafter,
    used,
    token,
    language,
    uniform,
    tiles,
    shares,
    send,
    arrived,
    terms,
    peaks,
    stat,
    stats,
    load_sem,
    send_sem,
    recv_sem,
    stat_send,
    stat_recv,
):
    me = lax.axis_index("tensor")
    barrier = pltpu.get_barrier_semaphore()
    for k in ORDER:
        peer = lax.rem(me + k, GROUP)
        pl.semaphore_signal(barrier, inc=1, device_id={"tensor": peer}, device_id_type=MESH)

    loads = []
    for at, (src, dst) in enumerate(
        (
            (logits_in, logits),
            (language_in, language),
            (drafter_in, drafter),
            (token_in, token),
            (uniform_in, uniform),
            (used_in, used),
            (q_in, q),
            (kv_in, kv),
            (fresh_in, fresh),
        )
    ):
        copy = pltpu.make_async_copy(src, dst, load_sem.at[at])
        copy.start()
        loads.append(copy)

    loads[0].wait()
    spread(lambda at, n: logits[:, at : at + n], tiles, ABSENT)
    for s in range(GROUP):
        send[s] = tiles[pl.ds(s, CHUNKS, stride=GROUP), :].astype(jnp.bfloat16)
    pl.semaphore_wait(barrier, GROUP - 1)
    copies = {}
    for k in ORDER:
        peer = lax.rem(me + k, GROUP)
        copy = pltpu.make_async_remote_copy(
            src_ref=send.at[peer],
            dst_ref=arrived.at[k],
            send_sem=send_sem.at[k],
            recv_sem=recv_sem.at[k],
            device_id={"tensor": peer},
            device_id_type=MESH,
        )
        copy.start()
        copies[k] = copy
    arrived[0] = send[me]

    for copy in loads[1:]:
        copy.wait()
    lang = language[me // 4]
    spread(lambda at, n: drafter[0, lang, :, at : at + n], shares, 0.0)
    total = jnp.sum(shares[...].reshape(CHUNKS * GROUP // 8, 8, LANES), axis=0)
    total = jnp.sum(total, axis=(0, 1), keepdims=True)
    inverse = 1.0 / total

    for r in range(4):
        attn_out[r] = attend(r, q, kv, fresh, used[r])

    place = lax.broadcasted_iota(jnp.int32, (CHUNKS, LANES), 0) * LANES + lax.broadcasted_iota(
        jnp.int32, (CHUNKS, LANES), 1
    )
    wanted = token[me]
    for k in (0,) + ORDER[::-1]:
        if k:
            copies[k].wait_recv()
        block = arrived[k].astype(jnp.float32).reshape(8, 8, LANES)
        peak = jnp.max(block, axis=0)
        peaks[k] = peak
        terms[k] = jnp.exp(block - peak[None])

    top = jnp.max(peaks[...], axis=0)
    top = jnp.max(top, axis=(0, 1), keepdims=True)
    norm = jnp.zeros((8, LANES), jnp.float32)
    for k in range(GROUP):
        norm = norm + jnp.sum(terms[k], axis=0) * jnp.exp(peaks[k] - top)
    norm = jnp.sum(norm, axis=(0, 1), keepdims=True)
    mass = jnp.zeros((8, LANES), jnp.float32)
    prob = jnp.zeros((8, LANES), jnp.float32)
    share = jnp.zeros((8, LANES), jnp.float32)
    for k in range(GROUP):
        piece = lax.rem(me + GROUP - k, GROUP)
        probs = terms[k] * (jnp.exp(peaks[k] - top) / norm)[None]
        drafted = shares[pl.ds(piece, CHUNKS, stride=GROUP), :].reshape(8, 8, LANES) * inverse[None]
        mass = mass + jnp.sum(jnp.maximum(probs - drafted, 0.0), axis=0)
        hit = (place == wanted - piece * VSHARD).reshape(8, 8, LANES)
        prob = prob + jnp.sum(jnp.where(hit, probs, 0.0), axis=0)
        share = share + jnp.sum(jnp.where(hit, drafted, 0.0), axis=0)
    mass = jnp.sum(mass, axis=(0, 1), keepdims=True)
    prob = jnp.sum(prob, axis=(0, 1), keepdims=True)
    share = jnp.sum(share, axis=(0, 1), keepdims=True)
    margin = jnp.minimum(1.0, prob / share) - uniform[me]

    lane = lax.broadcasted_iota(jnp.int32, (1, LANES), 1)
    row = jnp.where(lane == me, margin, 0.0) + jnp.where(lane == me + GROUP, mass, 0.0)
    stat[...] = row
    stat_copies = []
    for k in ORDER:
        peer = lax.rem(me + k, GROUP)
        copy = pltpu.make_async_remote_copy(
            src_ref=stat,
            dst_ref=stats.at[k - 1],
            send_sem=stat_send.at[k],
            recv_sem=stat_recv.at[k],
            device_id={"tensor": peer},
            device_id_type=MESH,
        )
        copy.start()
        stat_copies.append(copy)
    for k in ORDER:
        copies[k].wait_send()
    for copy in stat_copies:
        copy.wait()
    row = row + jnp.sum(stats[...], axis=0)
    margin_out[...] = row[0, 0:GROUP]
    mass_out[...] = row[0, GROUP : 2 * GROUP]


def on_device(
    queries, cache, new_kv, cache_len, target_logits, drafter, draft_tokens, language, uniforms
):
    anywhere = pl.BlockSpec(memory_space=pltpu.HBM)
    vmem = pl.BlockSpec(memory_space=pltpu.VMEM)
    f32 = jnp.float32
    bf16 = jnp.bfloat16
    return pl.pallas_call(
        kernel,
        out_shape=(
            jax.ShapeDtypeStruct(queries.shape, bf16),
            jax.ShapeDtypeStruct((GROUP,), f32),
            jax.ShapeDtypeStruct((GROUP,), f32),
        ),
        in_specs=[anywhere] * 9,
        out_specs=(vmem, vmem, vmem),
        scratch_shapes=[
            pltpu.VMEM(queries.shape, bf16),
            pltpu.VMEM(cache.shape, bf16),
            pltpu.VMEM(new_kv.shape, bf16),
            pltpu.VMEM(target_logits.shape, bf16),
            pltpu.VMEM(drafter.shape, bf16),
            pltpu.SMEM(cache_len.shape, jnp.int32),
            pltpu.SMEM(draft_tokens.shape, jnp.int32),
            pltpu.SMEM(language.shape, jnp.int32),
            pltpu.SMEM(uniforms.shape, f32),
            pltpu.VMEM((CHUNKS * GROUP, LANES), f32),
            pltpu.VMEM((CHUNKS * GROUP, LANES), f32),
            pltpu.VMEM((GROUP, CHUNKS, LANES), bf16),
            pltpu.VMEM((GROUP, CHUNKS, LANES), bf16),
            pltpu.VMEM((GROUP, 8, 8, LANES), f32),
            pltpu.VMEM((GROUP, 8, LANES), f32),
            pltpu.VMEM((1, LANES), f32),
            pltpu.VMEM((GROUP - 1, 1, LANES), f32),
            pltpu.SemaphoreType.DMA((9,)),
            pltpu.SemaphoreType.DMA((GROUP,)),
            pltpu.SemaphoreType.DMA((GROUP,)),
            pltpu.SemaphoreType.DMA((GROUP,)),
            pltpu.SemaphoreType.DMA((GROUP,)),
        ],
        compiler_params=pltpu.CompilerParams(
            collective_id=0, has_side_effects=True, vmem_limit_bytes=32 * 1024 * 1024
        ),
    )(queries, cache, new_kv, cache_len, target_logits, drafter, draft_tokens, language, uniforms)


def solution(mesh):
    in_specs = (
        P("dp", None, "tensor", None),
        P("tensor", "dp", None, None),
        P("tensor", "dp", None, None),
        P("dp"),
        P("dp", "tensor"),
        P(("dp", "tensor"), None, None, None),
        P("dp"),
        P("dp"),
        P("dp"),
    )
    out_specs = (P("dp", None, "tensor", None), P("dp"), P("dp"))
    return jax.shard_map(
        on_device, mesh=mesh, in_specs=in_specs, out_specs=out_specs, check_vma=False
    )
```

time: 124 us -> 36.1 us (0.29)
  blocking collectives: 101 us -> 0 us
  Pallas kernels: 0 us -> 26.3 us
  starting transfers between devices: 12 us -> 0 us
  local copies, waits for them, and re-layouts: 5.86 us -> 8.73 us
  other arithmetic: 2.22 us -> 0 us
  matrix products: 1.6 us -> 0 us
    pmax x2 -> x0, blocking collectives: 52.5 us -> none  [on_device(): row_peak, draft_logit = lax.pmax((local_peak, local_draft), 'tensor')]
    psum x2 -> x0, blocking collectives: 48.5 us -> none  [on_device(): lax.psum((jnp.sum(exp_terms, axis=1), weight_local, weight_draft_local),...]
    pallas_call x0 -> x1, Pallas kernels: none -> 26.3 us  [on_device(): pl.pallas_call(kernel, out_shape=(jax.ShapeDtypeStruct(queries.shape, bf1...]
    all_to_all x1 -> x0, starting transfers between devices: 12 us -> none  [on_device(): lax.all_to_all(drafter, 'tensor', split_axis=2, concat_axis=2, tiled=True)]
    unnamed x17 -> x21, local copies, waits for them, and re-layouts: 4.98 us -> 8.73 us
    dot_general x4 -> x0, matrix products: 1.6 us -> none  [the longest x1 0.83 us: attend(): jnp.einsum('rgikj,grjd->rigkd', fresh_w, new_kv[..., head_depth:], prefer...]
    reduce_sum x5 -> x0, other arithmetic: 1.41 us -> none  [the longest x1 0.52 us: on_device(): jnp.sum(jnp.maximum(target_probs - drafted, 0.0), axis=1)]
  transfers between devices with their start and end apart: 1 -> 0, of which waited for: 0 -> 0; matrix products, arithmetic and copies ran while one was open for 2% -> 0% of each run, Pallas kernels for 0% -> 0%
where the time goes in v1:
time: 36.1 us; the launch traced here: 35.7 us
  Pallas kernels  26.3 us (73%)
  local copies, waits for them, and re-layouts  8.73 us (24%)
  between operations  0.66 us (2%)
    pallas_call x1, Pallas kernels, on_device(): pl.pallas_call(kernel, out_shape=(jax.ShapeDtypeStruct(queries.shape, bf1...  26.3 us
    unnamed x21, local copies, waits for them, and re-layouts  8.73 us

profile of v1, /device:TPU:1, one launch (start us, length us, event | category | flops | bytes accessed | tf_op | source)
XLA Modules:
  0.0 35.7 jit_solution(7197969373300440619)
XLA Ops:
  0.6 0.0 copy-start
  0.6 1.0 %copy-done = bf16[1,4,256,256]{3,2,1,0:T(8,128)(2,1)S(1)} copy-done((bf16[1,4,256,256]{3,2,1,0:T(8,128)(2,1)S(1)}, bf16[1,4,256,256]{3,2,1,0:T(8,128)(2,1)}, u32[]{:S(2)}) %copy-start) | copy-done | bytes 524312
  1.7 0.0 copy-start.1
  1.7 1.0 %copy-done.1 = bf16[1,2,16,8016]{3,2,1,0:T(8,128)(2,1)S(1)} copy-done((bf16[1,2,16,8016]{3,2,1,0:T(8,128)(2,1)S(1)}, bf16[1,2,16,8016]{3,2,1,0:T(8,128)(2,1)}, u32[]{:S(2)}) %copy-start.1) | copy-done | bytes 513048
  2.7 0.0 copy-start.2
  2.7 0.9 %copy-done.2 = bf16[16,8016]{1,0:T(8,128)(2,1)S(1)} copy-done((bf16[16,8016]{1,0:T(8,128)(2,1)S(1)}, bf16[16,8016]{1,0:T(8,128)(2,1)}, u32[]{:S(2)}) %copy-start.2) | copy-done | bytes 256536
  3.7 0.0 copy-start.3
  3.7 0.8 %copy-done.3 = bf16[4,4,8,128]{3,2,1,0:T(8,128)(2,1)S(1)} copy-done((bf16[4,4,8,128]{3,2,1,0:T(8,128)(2,1)S(1)}, bf16[4,4,8,128]{3,2,1,0:T(8,128)(2,1)}, u32[]{:S(2)}) %copy-start.3) | copy-done | bytes 32792
  4.4 0.0 copy-start.4
  4.4 0.7 %copy-done.4 = bf16[1,4,4,256]{3,2,1,0:T(4,128)(2,1)S(1)} copy-done((bf16[1,4,4,256]{3,2,1,0:T(4,128)(2,1)S(1)}, bf16[1,4,4,256]{3,2,1,0:T(4,128)(2,1)}, u32[]{:S(2)}) %copy-start.4) | copy-done | bytes 8216
  5.1 0.0 copy-start.5
  5.1 0.7 %copy-done.5 = s32[4]{0:T(128)S(1)} copy-done((s32[4]{0:T(128)S(1)}, s32[4]{0:T(128)}, u32[]{:S(2)}) %copy-start.5) | copy-done | bytes 40
  5.8 0.0 copy-start.6
  5.8 0.7 %copy-done.6 = s32[16]{0:T(128)S(1)} copy-done((s32[16]{0:T(128)S(1)}, s32[16]{0:T(128)}, u32[]{:S(2)}) %copy-start.6) | copy-done | bytes 88
  6.4 0.0 copy-start.7
  6.4 0.7 %copy-done.7 = s32[4]{0:T(128)S(1)} copy-done((s32[4]{0:T(128)S(1)}, s32[4]{0:T(128)}, u32[]{:S(2)}) %copy-start.7) | copy-done | bytes 40
  7.1 0.0 copy-start.8
  7.1 0.7 %copy-done.8 = f32[16]{0:T(128)S(1)} copy-done((f32[16]{0:T(128)S(1)}, f32[16]{0:T(128)}, u32[]{:S(2)}) %copy-start.8) | copy-done | bytes 88
  7.7 26.3 %shard_map.112 = (bf16[4,4,8,128]{3,2,1,0:T(8,128)(2,1)S(1)}, f32[16]{0:T(128)S(1)}, f32[16]{0:T(128)S(1)}) custom-call(bf16[4,4,8,128]{3,2,1,0:T(8,128)(2,1)S(1)} %copy-done.3, bf16[1,4,256,256]{3,2,1,0:T(8,128)(2,1)S(1)} %copy-done, bf16[1,4,4,256]{3,2,1,0:T(4,128)(2,1)S(1)} %copy-done.4, s32[4]{0:T(128)S(1)} %copy-done.5, bf16[16,8016]{1,0:T(8,128)(2,1)S(1)} %copy-done.2, ...), custom_call_target="tpu_custom_call" | custom-call | tf_op jit(solution)/shard_map/pallas_call | solution.py:218
  34.1 0.6 %copy.15 = bf16[4,4,8,128]{3,2,1,0:T(8,128)(2,1)} copy(bf16[4,4,8,128]{3,2,1,0:T(8,128)(2,1)S(1)} %get-tuple-element.6) | data formatting | bytes 65536
  34.7 0.5 %copy.16 = f32[16]{0:T(128)} copy(f32[16]{0:T(128)S(1)} %get-tuple-element.7) | data formatting | bytes 128
  35.2 0.5 %copy.17 = f32[16]{0:T(128)} copy(f32[16]{0:T(128)S(1)} %get-tuple-element.8) | data formatting | bytes 128
Async XLA Ops:
  0.6 1.0 %copy-start = (bf16[1,4,256,256]{3,2,1,0:T(8,128)(2,1)S(1)}, bf16[1,4,256,256]{3,2,1,0:T(8,128)(2,1)}, u32[]{:S(2)}) copy-start(bf16[1,4,256,256]{3,2,1,0:T(8,128)(2,1)} %kv_in.1) | copy-start | bytes 1572868
  1.7 1.0 %copy-start.1 = (bf16[1,2,16,8016]{3,2,1,0:T(8,128)(2,1)S(1)}, bf16[1,2,16,8016]{3,2,1,0:T(8,128)(2,1)}, u32[]{:S(2)}) copy-start(bf16[1,2,16,8016]{3,2,1,0:T(8,128)(2,1)} %drafter_in.1) | copy-start | bytes 1539076
  2.7 0.9 %copy-start.2 = (bf16[16,8016]{1,0:T(8,128)(2,1)S(1)}, bf16[16,8016]{1,0:T(8,128)(2,1)}, u32[]{:S(2)}) copy-start(bf16[16,8016]{1,0:T(8,128)(2,1)} %logits_in.1) | copy-start | bytes 769540
  3.7 0.8 %copy-start.3 = (bf16[4,4,8,128]{3,2,1,0:T(8,128)(2,1)S(1)}, bf16[4,4,8,128]{3,2,1,0:T(8,128)(2,1)}, u32[]{:S(2)}) copy-start(bf16[4,4,8,128]{3,2,1,0:T(8,128)(2,1)} %q_in.1) | copy-start | bytes 98308
  4.4 0.7 %copy-start.4 = (bf16[1,4,4,256]{3,2,1,0:T(4,128)(2,1)S(1)}, bf16[1,4,4,256]{3,2,1,0:T(4,128)(2,1)}, u32[]{:S(2)}) copy-start(bf16[1,4,4,256]{3,2,1,0:T(4,128)(2,1)} %fresh_in.1) | copy-start | bytes 24580
  5.1 0.7 %copy-start.5 = (s32[4]{0:T(128)S(1)}, s32[4]{0:T(128)}, u32[]{:S(2)}) copy-start(s32[4]{0:T(128)} %used_in.1) | copy-start | bytes 52
  5.8 0.7 %copy-start.6 = (s32[16]{0:T(128)S(1)}, s32[16]{0:T(128)}, u32[]{:S(2)}) copy-start(s32[16]{0:T(128)} %token_in.1) | copy-start | bytes 196
  6.4 0.7 %copy-start.7 = (s32[4]{0:T(128)S(1)}, s32[4]{0:T(128)}, u32[]{:S(2)}) copy-start(s32[4]{0:T(128)} %language_in.1) | copy-start | bytes 52
  7.1 0.7 %copy-start.8 = (f32[16]{0:T(128)S(1)}, f32[16]{0:T(128)}, u32[]{:S(2)}) copy-start(f32[16]{0:T(128)} %uniform_in.1) | copy-start | bytes 196

commit v2 on v1

--- a/solution.py
+++ b/solution.py
@@ -249,7 +249,7 @@
             pltpu.SemaphoreType.DMA((GROUP,)),
         ],
         compiler_params=pltpu.CompilerParams(
-            collective_id=0, has_side_effects=True, vmem_limit_bytes=32 * 1024 * 1024
+            collective_id=0, has_side_effects=True, vmem_limit_bytes=60 * 1024 * 1024
         ),
     )(queries, cache, new_kv, cache_len, target_logits, drafter, draft_tokens, language, uniforms)
 

time: 36.1 us -> 30.2 us (0.84)
  local copies, waits for them, and re-layouts: 8.73 us -> 2.49 us
  Pallas kernels: 26.3 us -> 26.9 us
    unnamed x21 -> x7, local copies, waits for them, and re-layouts: 8.73 us -> 2.49 us
    pallas_call x1, Pallas kernels: 26.3 us -> 26.9 us  [on_device(): pl.pallas_call(kernel, out_shape=(jax.ShapeDtypeStruct(queries.shape, bf1...]
where the time goes in v2:
time: 30.2 us; the launch traced here: 30 us
  Pallas kernels  26.9 us (89%)
  local copies, waits for them, and re-layouts  2.49 us (8%)
  between operations  0.65 us (2%)
    pallas_call x1, Pallas kernels, on_device(): pl.pallas_call(kernel, out_shape=(jax.ShapeDtypeStruct(queries.shape, bf1...  26.9 us
    unnamed x7, local copies, waits for them, and re-layouts  2.49 us

profile of v2, /device:TPU:1, one launch (start us, length us, event | category | flops | bytes accessed | tf_op | source)
XLA Modules:
  0.0 30.0 jit_solution(6097122560966946366)
XLA Ops:
  0.6 26.9 %shard_map.112 = (bf16[4,4,8,128]{3,2,1,0:T(8,128)(2,1)}, f32[16]{0:T(128)}, f32[16]{0:T(128)}) custom-call(bf16[4,4,8,128]{3,2,1,0:T(8,128)(2,1)} %q_in.1, bf16[1,4,256,256]{3,2,1,0:T(8,128)(2,1)} %kv_in.1, bf16[1,4,4,256]{3,2,1,0:T(4,128)(2,1)} %fresh_in.1, s32[4]{0:T(128)} %used_in.1, bf16[16,8016]{1,0:T(8,128)(2,1)} %logits_in.1, ...), custom_call_target="tpu_custom_call" | custom-call | tf_op jit(solution)/shard_map/pallas_call | solution.py:218
  27.5 0.0 copy-start.1
  27.5 1.4 %copy.15 = bf16[4,4,8,128]{3,2,1,0:T(8,128)(2,1)} copy(bf16[4,4,8,128]{3,2,1,0:T(8,128)(2,1)} %get-tuple-element.6) | data formatting | bytes 65536
  28.9 0.0 copy-done.1
  28.9 0.0 copy-start
  28.9 0.5 %copy.16 = f32[16]{0:T(128)} copy(f32[16]{0:T(128)S(1)} %copy-done.1) | data formatting | bytes 128
  29.4 0.1 copy-done
  29.5 0.5 %copy.17 = f32[16]{0:T(128)} copy(f32[16]{0:T(128)S(1)} %copy-done) | data formatting | bytes 128
Async XLA Ops:
  27.5 1.4 %copy-start.1 = (f32[16]{0:T(128)S(1)}, f32[16]{0:T(128)}, u32[]{:S(2)}) copy-start(f32[16]{0:T(128)} %get-tuple-element.7) | copy-start | bytes 196
  28.9 0.6 %copy-start = (f32[16]{0:T(128)S(1)}, f32[16]{0:T(128)}, u32[]{:S(2)}) copy-start(f32[16]{0:T(128)} %get-tuple-element.8) | copy-start | bytes 196

commit v3 on v2

--- a/solution.py
+++ b/solution.py
@@ -15,7 +15,6 @@
 TAIL = VSHARD - FULL * LANES
 CHUNKS = 64
 ABSENT = -3.0e38
-ORDER = (8, 9, 7, 10, 6, 11, 5, 12, 4, 13, 3, 14, 2, 15, 1)
 
 
 def spread(load, tiles, fill):
@@ -69,8 +68,7 @@
     language_in,
     uniform_in,
     attn_out,
-    margin_out,
-    mass_out,
+    row_out,
     q,
     kv,
     fresh,
@@ -86,19 +84,31 @@
     arrived,
     terms,
     peaks,
-    stat,
+    norms,
+    picks,
     stats,
     load_sem,
     send_sem,
     recv_sem,
     stat_send,
     stat_recv,
+    ready,
 ):
     me = lax.axis_index("tensor")
+    shift = jnp.where(lax.axis_index("dp") == 0, 1, 0)
+    turn = lax.rem(me + (GROUP - 1) * shift, GROUP)
+
+    def rank_at(turn):
+        return lax.rem(turn + shift, GROUP)
+
     barrier = pltpu.get_barrier_semaphore()
-    for k in ORDER:
-        peer = lax.rem(me + k, GROUP)
+
+    def greet(at, carry):
+        peer = rank_at(at)
         pl.semaphore_signal(barrier, inc=1, device_id={"tensor": peer}, device_id_type=MESH)
+        return carry
+
+    lax.fori_loop(turn + 1, GROUP, greet, 0)
 
     loads = []
     for at, (src, dst) in enumerate(
@@ -115,97 +125,159 @@
         )
     ):
         copy = pltpu.make_async_copy(src, dst, load_sem.at[at])
+        if at == 0:
+            copy.start()
+        loads.append(copy)
+
+    @pl.when(turn > 0)
+    def _():
+        pl.semaphore_wait(barrier, turn)
+
+    def announce(at, carry):
+        peer = rank_at(at)
+        pl.semaphore_signal(ready.at[me], inc=1, device_id={"tensor": peer}, device_id_type=MESH)
+        return carry
+
+    lax.fori_loop(0, turn, announce, 0)
+    for copy in loads[1:]:
         copy.start()
-        loads.append(copy)
 
     loads[0].wait()
     spread(lambda at, n: logits[:, at : at + n], tiles, ABSENT)
     for s in range(GROUP):
         send[s] = tiles[pl.ds(s, CHUNKS, stride=GROUP), :].astype(jnp.bfloat16)
-    pl.semaphore_wait(barrier, GROUP - 1)
-    copies = {}
-    for k in ORDER:
-        peer = lax.rem(me + k, GROUP)
-        copy = pltpu.make_async_remote_copy(
+
+    def block_to(peer):
+        return pltpu.make_async_remote_copy(
             src_ref=send.at[peer],
-            dst_ref=arrived.at[k],
-            send_sem=send_sem.at[k],
-            recv_sem=recv_sem.at[k],
+            dst_ref=arrived.at[me],
+            send_sem=send_sem.at[peer],
+            recv_sem=recv_sem.at[me],
             device_id={"tensor": peer},
             device_id_type=MESH,
         )
-        copy.start()
-        copies[k] = copy
-    arrived[0] = send[me]
+
+    def block_from(peer):
+        return pltpu.make_async_remote_copy(
+            src_ref=send.at[peer],
+            dst_ref=arrived.at[peer],
+            send_sem=send_sem.at[peer],
+            recv_sem=recv_sem.at[peer],
+            device_id={"tensor": peer},
+            device_id_type=MESH,
+        )
+
+    def send_down(at, carry):
+        block_to(rank_at(at)).start()
+        return carry
+
+    lax.fori_loop(0, turn, send_down, 0)
+    arrived[me] = send[me]
 
     for copy in loads[1:]:
         copy.wait()
     lang = language[me // 4]
-    spread(lambda at, n: drafter[0, lang, :, at : at + n], shares, 0.0)
-    total = jnp.sum(shares[...].reshape(CHUNKS * GROUP // 8, 8, LANES), axis=0)
-    total = jnp.sum(total, axis=(0, 1), keepdims=True)
-    inverse = 1.0 / total
+    spread(lambda at, n: drafter[0, lang, :, at : at + n], tiles, 0.0)
+    total = jnp.sum(tiles[...].reshape(CHUNKS * GROUP // 8, 8, LANES), axis=0)
+    inverse = 1.0 / jnp.sum(total, axis=(0, 1), keepdims=True)
+    place = lax.broadcasted_iota(jnp.int32, (CHUNKS, LANES), 0) * LANES + lax.broadcasted_iota(
+        jnp.int32, (CHUNKS, LANES), 1
+    )
+    wanted = token[me]
+    share = jnp.zeros((8, LANES), jnp.float32)
+    for p in range(GROUP):
+        drafted = tiles[pl.ds(p, CHUNKS, stride=GROUP), :] * inverse
+        hit = place == wanted - p * VSHARD
+        share = share + jnp.sum(jnp.where(hit, drafted, 0.0).reshape(8, 8, LANES), axis=0)
+        shares[p] = drafted.reshape(8, 8, LANES)
+    share = jnp.sum(share, axis=(0, 1), keepdims=True)
 
     for r in range(4):
         attn_out[r] = attend(r, q, kv, fresh, used[r])
 
-    place = lax.broadcasted_iota(jnp.int32, (CHUNKS, LANES), 0) * LANES + lax.broadcasted_iota(
-        jnp.int32, (CHUNKS, LANES), 1
-    )
-    wanted = token[me]
-    for k in (0,) + ORDER[::-1]:
-        if k:
-            copies[k].wait_recv()
-        block = arrived[k].astype(jnp.float32).reshape(8, 8, LANES)
+    def send_up(at, carry):
+        peer = rank_at(at)
+        pl.semaphore_wait(ready.at[peer], 1)
+        block_to(peer).start()
+        return carry
+
+    lax.fori_loop(turn + 1, GROUP, send_up, 0)
+
+    def digest(peer):
+        block = arrived[peer].astype(jnp.float32).reshape(8, 8, LANES)
         peak = jnp.max(block, axis=0)
-        peaks[k] = peak
-        terms[k] = jnp.exp(block - peak[None])
+        term = jnp.exp(block - peak[None])
+        hit = (place == wanted - peer * VSHARD).reshape(8, 8, LANES)
+        peaks[peer] = peak
+        terms[peer] = term
+        norms[peer] = jnp.sum(term, axis=0)
+        picks[peer] = jnp.sum(jnp.where(hit, term, 0.0), axis=0)
+
+    def receive(at, carry):
+        peer = rank_at(at)
+        block_from(peer).wait_recv()
+        digest(peer)
+        return carry
+
+    digest(me)
+    lax.fori_loop(0, turn, receive, 0)
+    lax.fori_loop(turn + 1, GROUP, receive, 0)
 
     top = jnp.max(peaks[...], axis=0)
     top = jnp.max(top, axis=(0, 1), keepdims=True)
-    norm = jnp.zeros((8, LANES), jnp.float32)
-    for k in range(GROUP):
-        norm = norm + jnp.sum(terms[k], axis=0) * jnp.exp(peaks[k] - top)
-    norm = jnp.sum(norm, axis=(0, 1), keepdims=True)
+    scales = jnp.exp(peaks[...] - top[None])
+    norm = jnp.sum(norms[...] * scales, axis=0)
+    scales = scales * (1.0 / jnp.sum(norm, axis=(0, 1), keepdims=True))[None]
+    prob = jnp.sum(picks[...] * scales, axis=0)
     mass = jnp.zeros((8, LANES), jnp.float32)
-    prob = jnp.zeros((8, LANES), jnp.float32)
-    share = jnp.zeros((8, LANES), jnp.float32)
-    for k in range(GROUP):
-        piece = lax.rem(me + GROUP - k, GROUP)
-        probs = terms[k] * (jnp.exp(peaks[k] - top) / norm)[None]
-        drafted = shares[pl.ds(piece, CHUNKS, stride=GROUP), :].reshape(8, 8, LANES) * inverse[None]
-        mass = mass + jnp.sum(jnp.maximum(probs - drafted, 0.0), axis=0)
-        hit = (place == wanted - piece * VSHARD).reshape(8, 8, LANES)
-        prob = prob + jnp.sum(jnp.where(hit, probs, 0.0), axis=0)
-        share = share + jnp.sum(jnp.where(hit, drafted, 0.0), axis=0)
+    for p in range(GROUP):
+        mass = mass + jnp.sum(jnp.maximum(terms[p] * scales[p][None] - shares[p], 0.0), axis=0)
     mass = jnp.sum(mass, axis=(0, 1), keepdims=True)
     prob = jnp.sum(prob, axis=(0, 1), keepdims=True)
-    share = jnp.sum(share, axis=(0, 1), keepdims=True)
     margin = jnp.minimum(1.0, prob / share) - uniform[me]
 
     lane = lax.broadcasted_iota(jnp.int32, (1, LANES), 1)
     row = jnp.where(lane == me, margin, 0.0) + jnp.where(lane == me + GROUP, mass, 0.0)
-    stat[...] = row
-    stat_copies = []
-    for k in ORDER:
-        peer = lax.rem(me + k, GROUP)
-        copy = pltpu.make_async_remote_copy(
-            src_ref=stat,
-            dst_ref=stats.at[k - 1],
-            send_sem=stat_send.at[k],
-            recv_sem=stat_recv.at[k],
+    stats[me] = row
+
+    def stat_to(peer):
+        return pltpu.make_async_remote_copy(
+            src_ref=stats.at[me],
+            dst_ref=stats.at[me],
+            send_sem=stat_send.at[peer],
+            recv_sem=stat_recv.at[me],
             device_id={"tensor": peer},
             device_id_type=MESH,
         )
-        copy.start()
-        stat_copies.append(copy)
-    for k in ORDER:
-        copies[k].wait_send()
-    for copy in stat_copies:
-        copy.wait()
-    row = row + jnp.sum(stats[...], axis=0)
-    margin_out[...] = row[0, 0:GROUP]
-    mass_out[...] = row[0, GROUP : 2 * GROUP]
+
+    def stat_start(peer, carry):
+        stat_to(peer).start()
+        return carry
+
+    lax.fori_loop(0, me, stat_start, 0)
+    lax.fori_loop(me + 1, GROUP, stat_start, 0)
+
+    def sent(peer, carry):
+        block_to(peer).wait_send()
+        return carry
+
+    lax.fori_loop(0, me, sent, 0)
+    lax.fori_loop(me + 1, GROUP, sent, 0)
+
+    def stat_done(peer, carry):
+        pltpu.make_async_remote_copy(
+            src_ref=stats.at[me],
+            dst_ref=stats.at[peer],
+            send_sem=stat_send.at[peer],
+            recv_sem=stat_recv.at[peer],
+            device_id={"tensor": peer},
+            device_id_type=MESH,
+        ).wait()
+        return carry
+
+    lax.fori_loop(0, me, stat_done, 0)
+    lax.fori_loop(me + 1, GROUP, stat_done, 0)
+    row_out[...] = jnp.sum(stats[...], axis=0)
 
 
 def on_device(
@@ -215,15 +287,14 @@
     vmem = pl.BlockSpec(memory_space=pltpu.VMEM)
     f32 = jnp.float32
     bf16 = jnp.bfloat16
-    return pl.pallas_call(
+    attn, row = pl.pallas_call(
         kernel,
         out_shape=(
-            jax.ShapeDtypeStruct(queries.shape, bf16),
-            jax.ShapeDtypeStruct((GROUP,), f32),
-            jax.ShapeDtypeStruct((GROUP,), f32),
+            pltpu.VMEM(queries.shape, bf16),
+            pltpu.VMEM((1, LANES), f32),
         ),
         in_specs=[anywhere] * 9,
-        out_specs=(vmem, vmem, vmem),
+        out_specs=(vmem, vmem),
         scratch_shapes=[
             pltpu.VMEM(queries.shape, bf16),
             pltpu.VMEM(cache.shape, bf16),
@@ -235,23 +306,26 @@
             pltpu.SMEM(language.shape, jnp.int32),
             pltpu.SMEM(uniforms.shape, f32),
             pltpu.VMEM((CHUNKS * GROUP, LANES), f32),
-            pltpu.VMEM((CHUNKS * GROUP, LANES), f32),
+            pltpu.VMEM((GROUP, 8, 8, LANES), f32),
             pltpu.VMEM((GROUP, CHUNKS, LANES), bf16),
             pltpu.VMEM((GROUP, CHUNKS, LANES), bf16),
             pltpu.VMEM((GROUP, 8, 8, LANES), f32),
             pltpu.VMEM((GROUP, 8, LANES), f32),
-            pltpu.VMEM((1, LANES), f32),
-            pltpu.VMEM((GROUP - 1, 1, LANES), f32),
+            pltpu.VMEM((GROUP, 8, LANES), f32),
+            pltpu.VMEM((GROUP, 8, LANES), f32),
+            pltpu.VMEM((GROUP, 1, LANES), f32),
             pltpu.SemaphoreType.DMA((9,)),
             pltpu.SemaphoreType.DMA((GROUP,)),
             pltpu.SemaphoreType.DMA((GROUP,)),
             pltpu.SemaphoreType.DMA((GROUP,)),
             pltpu.SemaphoreType.DMA((GROUP,)),
+            pltpu.SemaphoreType.REGULAR((GROUP,)),
         ],
         compiler_params=pltpu.CompilerParams(
             collective_id=0, has_side_effects=True, vmem_limit_bytes=60 * 1024 * 1024
         ),
     )(queries, cache, new_kv, cache_len, target_logits, drafter, draft_tokens, language, uniforms)
+    return attn, row[0, :GROUP], row[0, GROUP : 2 * GROUP]
 
 
 def solution(mesh):

time: 30.2 us -> 27.1 us (0.90)
  Pallas kernels: 26.9 us -> 25.2 us
  local copies, waits for them, and re-layouts: 2.49 us -> 1.2 us
    unnamed x7 -> x1, local copies, waits for them, and re-layouts: 2.49 us -> 0.62 us
    pallas_call x1, Pallas kernels: 26.9 us -> 25.2 us  [on_device(): pl.pallas_call(kernel, out_shape=(pltpu.VMEM(queries.shape, bf16), pltpu....]
    squeeze x0 -> x1, local copies, waits for them, and re-layouts: none -> 0.58 us  [on_device(): return (attn, row[0, :GROUP], row[0, GROUP:2 * GROUP])]
where the time goes in v3:
time: 27.1 us; the launch traced here: 27 us
  Pallas kernels  25.2 us (93%)
  local copies, waits for them, and re-layouts  1.2 us (4%)
  between operations  0.64 us (2%)
    pallas_call x1, Pallas kernels, on_device(): pl.pallas_call(kernel, out_shape=(pltpu.VMEM(queries.shape, bf16), pltpu....  25.2 us
    unnamed x1, local copies, waits for them, and re-layouts  0.62 us
    squeeze x1, local copies, waits for them, and re-layouts, on_device(): return (attn, row[0, :GROUP], row[0, GROUP:2 * GROUP])  0.58 us

profile of v3, /device:TPU:1, one launch (start us, length us, event | category | flops | bytes accessed | tf_op | source)
XLA Modules:
  0.0 27.0 jit_solution(7580973132270689879)
XLA Ops:
  0.6 25.2 %shard_map.112 = (bf16[4,4,8,128]{3,2,1,0:T(8,128)(2,1)S(1)}, f32[1,128]{1,0:T(1,128)S(1)}) custom-call(bf16[4,4,8,128]{3,2,1,0:T(8,128)(2,1)} %q_in.1, bf16[1,4,256,256]{3,2,1,0:T(8,128)(2,1)} %kv_in.1, bf16[1,4,4,256]{3,2,1,0:T(4,128)(2,1)} %fresh_in.1, s32[4]{0:T(128)} %used_in.1, bf16[16,8016]{1,0:T(8,128)(2,1)} %logits_in.1, ...), custom_call_target="tpu_custom_call" | custom-call | tf_op jit(solution)/shard_map/pallas_call | solution.py:290
  25.8 0.6 %copy.13 = bf16[4,4,8,128]{3,2,1,0:T(8,128)(2,1)} copy(bf16[4,4,8,128]{3,2,1,0:T(8,128)(2,1)S(1)} %get-tuple-element.9) | data formatting | bytes 65536
  26.4 0.6 %slice_bitcast_fusion = (f32[16]{0:T(128)}, f32[16]{0:T(128)}) fusion(f32[1,128]{1,0:T(1,128)S(1)} %get-tuple-element.6), kind=kLoop, calls=%fused_computation | loop fusion | bytes 256 | tf_op jit(solution)/shard_map/squeeze | solution.py:328

commit v4 on v3

--- a/solution.py
+++ b/solution.py
@@ -101,6 +101,13 @@
     def rank_at(turn):
         return lax.rem(turn + shift, GROUP)
 
+    def far_first(at):
+        near = (at + 1) // 2
+        return lax.rem(me + 8 + near * (1 - 2 * ((at + 1) % 2)), GROUP)
+
+    def turn_of(rank):
+        return lax.rem(rank + (GROUP - 1) * shift, GROUP)
+
     barrier = pltpu.get_barrier_semaphore()
 
     def greet(at, carry):
@@ -134,18 +141,26 @@
         pl.semaphore_wait(barrier, turn)
 
     def announce(at, carry):
-        peer = rank_at(at)
-        pl.semaphore_signal(ready.at[me], inc=1, device_id={"tensor": peer}, device_id_type=MESH)
-        return carry
-
-    lax.fori_loop(0, turn, announce, 0)
+        peer = far_first(at)
+
+        @pl.when(turn_of(peer) < turn)
+        def _():
+            pl.semaphore_signal(
+                ready.at[me], inc=1, device_id={"tensor": peer}, device_id_type=MESH
+            )
+
+        return carry
+
+    lax.fori_loop(0, GROUP - 1, announce, 0)
     for copy in loads[1:]:
         copy.start()
 
     loads[0].wait()
     spread(lambda at, n: logits[:, at : at + n], tiles, ABSENT)
-    for s in range(GROUP):
-        send[s] = tiles[pl.ds(s, CHUNKS, stride=GROUP), :].astype(jnp.bfloat16)
+
+    def pack(slot):
+        send[slot] = tiles[pl.ds(slot, CHUNKS, stride=GROUP), :].astype(jnp.bfloat16)
+
 
     def block_to(peer):
         return pltpu.make_async_remote_copy(
@@ -168,11 +183,17 @@
         )
 
     def send_down(at, carry):
-        block_to(rank_at(at)).start()
-        return carry
-
-    lax.fori_loop(0, turn, send_down, 0)
-    arrived[me] = send[me]
+        peer = far_first(at)
+        pack(peer)
+
+        @pl.when(turn_of(peer) < turn)
+        def _():
+            block_to(peer).start()
+
+        return carry
+
+    lax.fori_loop(0, GROUP - 1, send_down, 0)
+    arrived[me] = tiles[pl.ds(me, CHUNKS, stride=GROUP), :].astype(jnp.bfloat16)
 
     for copy in loads[1:]:
         copy.wait()

time: 27.1 us -> 26 us (0.959)
  Pallas kernels: 25.2 us -> 24 us
    pallas_call x1, Pallas kernels: 25.2 us -> 24 us  [on_device(): pl.pallas_call(kernel, out_shape=(pltpu.VMEM(queries.shape, bf16), pltpu....]
where the time goes in v4:
time: 26 us; the launch traced here: 25.8 us
  Pallas kernels  24 us (92%)
  local copies, waits for them, and re-layouts  1.2 us (5%)
  between operations  0.64 us (2%)
    pallas_call x1, Pallas kernels, on_device(): pl.pallas_call(kernel, out_shape=(pltpu.VMEM(queries.shape, bf16), pltpu....  24 us
    unnamed x1, local copies, waits for them, and re-layouts  0.62 us
    squeeze x1, local copies, waits for them, and re-layouts, on_device(): return (attn, row[0, :GROUP], row[0, GROUP:2 * GROUP])  0.58 us

profile of v4, /device:TPU:1, one launch (start us, length us, event | category | flops | bytes accessed | tf_op | source)
XLA Modules:
  0.0 25.8 jit_solution(6178735424019044270)
XLA Ops:
  0.6 24.0 %shard_map.112 = (bf16[4,4,8,128]{3,2,1,0:T(8,128)(2,1)S(1)}, f32[1,128]{1,0:T(1,128)S(1)}) custom-call(bf16[4,4,8,128]{3,2,1,0:T(8,128)(2,1)} %q_in.1, bf16[1,4,256,256]{3,2,1,0:T(8,128)(2,1)} %kv_in.1, bf16[1,4,4,256]{3,2,1,0:T(4,128)(2,1)} %fresh_in.1, s32[4]{0:T(128)} %used_in.1, bf16[16,8016]{1,0:T(8,128)(2,1)} %logits_in.1, ...), custom_call_target="tpu_custom_call" | custom-call | tf_op jit(solution)/shard_map/pallas_call | solution.py:311
  24.6 0.6 %copy.13 = bf16[4,4,8,128]{3,2,1,0:T(8,128)(2,1)} copy(bf16[4,4,8,128]{3,2,1,0:T(8,128)(2,1)S(1)} %get-tuple-element.9) | data formatting | bytes 65536
  25.3 0.6 %slice_bitcast_fusion = (f32[16]{0:T(128)}, f32[16]{0:T(128)}) fusion(f32[1,128]{1,0:T(1,128)S(1)} %get-tuple-element.6), kind=kLoop, calls=%fused_computation | loop fusion | bytes 256 | tf_op jit(solution)/shard_map/squeeze | solution.py:349

commit v5 on v4

--- a/solution.py
+++ b/solution.py
@@ -120,7 +120,10 @@
     loads = []
     for at, (src, dst) in enumerate(
         (
-            (logits_in, logits),
+            (logits_in.at[:, :2048], logits.at[:, :2048]),
+            (logits_in.at[:, 2048:4096], logits.at[:, 2048:4096]),
+            (logits_in.at[:, 4096:6144], logits.at[:, 4096:6144]),
+            (logits_in.at[:, 6144:], logits.at[:, 6144:]),
             (language_in, language),
             (drafter_in, drafter),
             (token_in, token),
@@ -132,7 +135,7 @@
         )
     ):
         copy = pltpu.make_async_copy(src, dst, load_sem.at[at])
-        if at == 0:
+        if at < 4:
             copy.start()
         loads.append(copy)
 
@@ -152,11 +155,15 @@
         return carry
 
     lax.fori_loop(0, GROUP - 1, announce, 0)
-    for copy in loads[1:]:
+    for copy in loads[4:]:
         copy.start()
 
-    loads[0].wait()
-    spread(lambda at, n: logits[:, at : at + n], tiles, ABSENT)
+    def logit_tile(at, n):
+        if at % 2048 == 0:
+            loads[at // 2048].wait()
+        return logits[:, at : at + n]
+
+    spread(logit_tile, tiles, ABSENT)
 
     def pack(slot):
         send[slot] = tiles[pl.ds(slot, CHUNKS, stride=GROUP), :].astype(jnp.bfloat16)
@@ -195,7 +202,15 @@
     lax.fori_loop(0, GROUP - 1, send_down, 0)
     arrived[me] = tiles[pl.ds(me, CHUNKS, stride=GROUP), :].astype(jnp.bfloat16)
 
-    for copy in loads[1:]:
+    def send_up(at, carry):
+        peer = rank_at(at)
+        pl.semaphore_wait(ready.at[peer], 1)
+        block_to(peer).start()
+        return carry
+
+    lax.fori_loop(turn + 1, GROUP, send_up, 0)
+
+    for copy in loads[4:]:
         copy.wait()
     lang = language[me // 4]
     spread(lambda at, n: drafter[0, lang, :, at : at + n], tiles, 0.0)
@@ -215,14 +230,6 @@
 
     for r in range(4):
         attn_out[r] = attend(r, q, kv, fresh, used[r])
-
-    def send_up(at, carry):
-        peer = rank_at(at)
-        pl.semaphore_wait(ready.at[peer], 1)
-        block_to(peer).start()
-        return carry
-
-    lax.fori_loop(turn + 1, GROUP, send_up, 0)
 
     def digest(peer):
         block = arrived[peer].astype(jnp.float32).reshape(8, 8, LANES)
@@ -335,7 +342,7 @@
             pltpu.VMEM((GROUP, 8, LANES), f32),
             pltpu.VMEM((GROUP, 8, LANES), f32),
             pltpu.VMEM((GROUP, 1, LANES), f32),
-            pltpu.SemaphoreType.DMA((9,)),
+            pltpu.SemaphoreType.DMA((12,)),
             pltpu.SemaphoreType.DMA((GROUP,)),
             pltpu.SemaphoreType.DMA((GROUP,)),
             pltpu.SemaphoreType.DMA((GROUP,)),

time: 26 us -> 26 us (level)
  no operation moved by 1% of the time
where the time goes in v5:
time: 26 us; the launch traced here: 25.9 us
  Pallas kernels  24 us (92%)
  local copies, waits for them, and re-layouts  1.2 us (5%)
  between operations  0.64 us (2%)
    pallas_call x1, Pallas kernels, on_device(): pl.pallas_call(kernel, out_shape=(pltpu.VMEM(queries.shape, bf16), pltpu....  24 us
    unnamed x1, local copies, waits for them, and re-layouts  0.62 us
    squeeze x1, local copies, waits for them, and re-layouts, on_device(): return (attn, row[0, :GROUP], row[0, GROUP:2 * GROUP])  0.58 us

profile of v5, /device:TPU:1, one launch (start us, length us, event | category | flops | bytes accessed | tf_op | source)
XLA Modules:
  0.0 25.9 jit_solution(1220744183607815039)
XLA Ops:
  0.6 24.0 %shard_map.112 = (bf16[4,4,8,128]{3,2,1,0:T(8,128)(2,1)S(1)}, f32[1,128]{1,0:T(1,128)S(1)}) custom-call(bf16[4,4,8,128]{3,2,1,0:T(8,128)(2,1)} %q_in.1, bf16[1,4,256,256]{3,2,1,0:T(8,128)(2,1)} %kv_in.1, bf16[1,4,4,256]{3,2,1,0:T(4,128)(2,1)} %fresh_in.1, s32[4]{0:T(128)} %used_in.1, bf16[16,8016]{1,0:T(8,128)(2,1)} %logits_in.1, ...), custom_call_target="tpu_custom_call" | custom-call | tf_op jit(solution)/shard_map/pallas_call | solution.py:318
  24.7 0.6 %copy.13 = bf16[4,4,8,128]{3,2,1,0:T(8,128)(2,1)} copy(bf16[4,4,8,128]{3,2,1,0:T(8,128)(2,1)S(1)} %get-tuple-element.9) | data formatting | bytes 65536
  25.3 0.6 %slice_bitcast_fusion = (f32[16]{0:T(128)}, f32[16]{0:T(128)}) fusion(f32[1,128]{1,0:T(1,128)S(1)} %get-tuple-element.6), kind=kLoop, calls=%fused_computation | loop fusion | bytes 256 | tf_op jit(solution)/shard_map/squeeze | solution.py:356

commit v6 on v5

--- a/solution.py
+++ b/solution.py
@@ -241,15 +241,19 @@
         norms[peer] = jnp.sum(term, axis=0)
         picks[peer] = jnp.sum(jnp.where(hit, term, 0.0), axis=0)
 
-    def receive(at, carry):
+    def receive(step, carry):
+        at = lax.rem(step + me // 8 * (8 - shift), GROUP)
         peer = rank_at(at)
-        block_from(peer).wait_recv()
-        digest(peer)
+
+        @pl.when(at != turn)
+        def _():
+            block_from(peer).wait_recv()
+            digest(peer)
+
         return carry
 
     digest(me)
-    lax.fori_loop(0, turn, receive, 0)
-    lax.fori_loop(turn + 1, GROUP, receive, 0)
+    lax.fori_loop(0, GROUP, receive, 0)
 
     top = jnp.max(peaks[...], axis=0)
     top = jnp.max(top, axis=(0, 1), keepdims=True)

time: 26 us -> 25.9 us (level)
  no operation moved by 1% of the time
where the time goes in v6:
time: 25.9 us; the launch traced here: 25.7 us
  Pallas kernels  23.9 us (92%)
  local copies, waits for them, and re-layouts  1.2 us (5%)
  between operations  0.64 us (2%)
    pallas_call x1, Pallas kernels, on_device(): pl.pallas_call(kernel, out_shape=(pltpu.VMEM(queries.shape, bf16), pltpu....  23.9 us
    unnamed x1, local copies, waits for them, and re-layouts  0.62 us
    squeeze x1, local copies, waits for them, and re-layouts, on_device(): return (attn, row[0, :GROUP], row[0, GROUP:2 * GROUP])  0.58 us

profile of v6, /device:TPU:1, one launch (start us, length us, event | category | flops | bytes accessed | tf_op | source)
XLA Modules:
  0.0 25.7 jit_solution(15978793156541346271)
XLA Ops:
  0.6 23.9 %shard_map.112 = (bf16[4,4,8,128]{3,2,1,0:T(8,128)(2,1)S(1)}, f32[1,128]{1,0:T(1,128)S(1)}) custom-call(bf16[4,4,8,128]{3,2,1,0:T(8,128)(2,1)} %q_in.1, bf16[1,4,256,256]{3,2,1,0:T(8,128)(2,1)} %kv_in.1, bf16[1,4,4,256]{3,2,1,0:T(4,128)(2,1)} %fresh_in.1, s32[4]{0:T(128)} %used_in.1, bf16[16,8016]{1,0:T(8,128)(2,1)} %logits_in.1, ...), custom_call_target="tpu_custom_call" | custom-call | tf_op jit(solution)/shard_map/pallas_call | solution.py:322
  24.5 0.6 %copy.13 = bf16[4,4,8,128]{3,2,1,0:T(8,128)(2,1)} copy(bf16[4,4,8,128]{3,2,1,0:T(8,128)(2,1)S(1)} %get-tuple-element.9) | data formatting | bytes 65536
  25.2 0.6 %slice_bitcast_fusion = (f32[16]{0:T(128)}, f32[16]{0:T(128)}) fusion(f32[1,128]{1,0:T(1,128)S(1)} %get-tuple-element.6), kind=kLoop, calls=%fused_computation | loop fusion | bytes 256 | tf_op jit(solution)/shard_map/squeeze | solution.py:360

commit v7 on v5

--- a/solution.py
+++ b/solution.py
@@ -240,18 +240,17 @@
         terms[peer] = term
         norms[peer] = jnp.sum(term, axis=0)
         picks[peer] = jnp.sum(jnp.where(hit, term, 0.0), axis=0)
-
-    def receive(at, carry):
+        return peak
+
+    first = me // 8 * (8 - shift)
+
+    def receive(step, top):
+        at = lax.rem(first + step + jnp.where(step >= turn - first, 1, 0), GROUP)
         peer = rank_at(at)
         block_from(peer).wait_recv()
-        digest(peer)
-        return carry
-
-    digest(me)
-    lax.fori_loop(0, turn, receive, 0)
-    lax.fori_loop(turn + 1, GROUP, receive, 0)
-
-    top = jnp.max(peaks[...], axis=0)
+        return jnp.maximum(top, digest(peer))
+
+    top = lax.fori_loop(0, GROUP - 1, receive, digest(me))
     top = jnp.max(top, axis=(0, 1), keepdims=True)
     scales = jnp.exp(peaks[...] - top[None])
     norm = jnp.sum(norms[...] * scales, axis=0)

time: 26 us -> 25.8 us (level)
  no operation moved by 1% of the time
where the time goes in v7:
time: 25.8 us; the launch traced here: 25.7 us
  Pallas kernels  23.8 us (92%)
  local copies, waits for them, and re-layouts  1.2 us (5%)
  between operations  0.64 us (2%)
    pallas_call x1, Pallas kernels, on_device(): pl.pallas_call(kernel, out_shape=(pltpu.VMEM(queries.shape, bf16), pltpu....  23.8 us
    unnamed x1, local copies, waits for them, and re-layouts  0.62 us
    squeeze x1, local copies, waits for them, and re-layouts, on_device(): return (attn, row[0, :GROUP], row[0, GROUP:2 * GROUP])  0.58 us

profile of v7, /device:TPU:1, one launch (start us, length us, event | category | flops | bytes accessed | tf_op | source)
XLA Modules:
  0.0 25.7 jit_solution(18299422331109998976)
XLA Ops:
  0.6 23.8 %shard_map.112 = (bf16[4,4,8,128]{3,2,1,0:T(8,128)(2,1)S(1)}, f32[1,128]{1,0:T(1,128)S(1)}) custom-call(bf16[4,4,8,128]{3,2,1,0:T(8,128)(2,1)} %q_in.1, bf16[1,4,256,256]{3,2,1,0:T(8,128)(2,1)} %kv_in.1, bf16[1,4,4,256]{3,2,1,0:T(4,128)(2,1)} %fresh_in.1, s32[4]{0:T(128)} %used_in.1, bf16[16,8016]{1,0:T(8,128)(2,1)} %logits_in.1, ...), custom_call_target="tpu_custom_call" | custom-call | tf_op jit(solution)/shard_map/pallas_call | solution.py:317
  24.5 0.6 %copy.13 = bf16[4,4,8,128]{3,2,1,0:T(8,128)(2,1)} copy(bf16[4,4,8,128]{3,2,1,0:T(8,128)(2,1)S(1)} %get-tuple-element.9) | data formatting | bytes 65536
  25.1 0.6 %slice_bitcast_fusion = (f32[16]{0:T(128)}, f32[16]{0:T(128)}) fusion(f32[1,128]{1,0:T(1,128)S(1)} %get-tuple-element.6), kind=kLoop, calls=%fused_computation | loop fusion | bytes 256 | tf_op jit(solution)/shard_map/squeeze | solution.py:355

commit v8 on v7

--- a/solution.py
+++ b/solution.py
@@ -203,12 +203,17 @@
     arrived[me] = tiles[pl.ds(me, CHUNKS, stride=GROUP), :].astype(jnp.bfloat16)
 
     def send_up(at, carry):
+        at = at + (at // 8) * (4 * ((at % 8) // 4) + 2 * (at % 2) + (at % 4) // 2 - at % 8)
         peer = rank_at(at)
-        pl.semaphore_wait(ready.at[peer], 1)
-        block_to(peer).start()
-        return carry
-
-    lax.fori_loop(turn + 1, GROUP, send_up, 0)
+
+        @pl.when(at > turn)
+        def _():
+            pl.semaphore_wait(ready.at[peer], 1)
+            block_to(peer).start()
+
+        return carry
+
+    lax.fori_loop(0, GROUP, send_up, 0)
 
     for copy in loads[4:]:
         copy.wait()

time: 25.8 us -> 25.6 us (level)
  no operation moved by 1% of the time
where the time goes in v8:
time: 25.6 us; the launch traced here: 25.5 us
  Pallas kernels  23.6 us (92%)
  local copies, waits for them, and re-layouts  1.2 us (5%)
  between operations  0.64 us (2%)
    pallas_call x1, Pallas kernels, on_device(): pl.pallas_call(kernel, out_shape=(pltpu.VMEM(queries.shape, bf16), pltpu....  23.6 us
    unnamed x1, local copies, waits for them, and re-layouts  0.62 us
    squeeze x1, local copies, waits for them, and re-layouts, on_device(): return (attn, row[0, :GROUP], row[0, GROUP:2 * GROUP])  0.58 us

profile of v8, /device:TPU:1, one launch (start us, length us, event | category | flops | bytes accessed | tf_op | source)
XLA Modules:
  0.0 25.5 jit_solution(16425108235469822234)
XLA Ops:
  0.6 23.6 %shard_map.112 = (bf16[4,4,8,128]{3,2,1,0:T(8,128)(2,1)S(1)}, f32[1,128]{1,0:T(1,128)S(1)}) custom-call(bf16[4,4,8,128]{3,2,1,0:T(8,128)(2,1)} %q_in.1, bf16[1,4,256,256]{3,2,1,0:T(8,128)(2,1)} %kv_in.1, bf16[1,4,4,256]{3,2,1,0:T(4,128)(2,1)} %fresh_in.1, s32[4]{0:T(128)} %used_in.1, bf16[16,8016]{1,0:T(8,128)(2,1)} %logits_in.1, ...), custom_call_target="tpu_custom_call" | custom-call | tf_op jit(solution)/shard_map/pallas_call | solution.py:322
  24.3 0.6 %copy.13 = bf16[4,4,8,128]{3,2,1,0:T(8,128)(2,1)} copy(bf16[4,4,8,128]{3,2,1,0:T(8,128)(2,1)S(1)} %get-tuple-element.9) | data formatting | bytes 65536
  24.9 0.6 %slice_bitcast_fusion = (f32[16]{0:T(128)}, f32[16]{0:T(128)}) fusion(f32[1,128]{1,0:T(1,128)S(1)} %get-tuple-element.6), kind=kLoop, calls=%fused_computation | loop fusion | bytes 256 | tf_op jit(solution)/shard_map/squeeze | solution.py:360
